TPU v7x, 32 devices: a whole 2x2x4 slice. The times are simulated.
32 devices in a mesh: member: 2 (over y), lon: 8 (over z, x), lat: 2 (over core).
Axes of the slice: x: 2, y: 2, z: 4, core: 2. Of those that a mesh axis runs over, the one named last changes fastest.
Arguments:
- innovation: float32 [65536], P(('member', 'lon', 'lat')), parts along dimension 0, may hold values from -6 to 6
- fractions: float32 [3, 65536], P(None, ('member', 'lon', 'lat')), parts along dimension 1, may hold values from 0 to 1
- owner: int32 [65536, 1], P(('member', 'lon', 'lat')), parts along dimension 0, may hold values from 0 to 15; in each aligned block of 2048 rows (0 to 2047, 2048 to 4095, ...) at most 256 rows name the same one
- obs_row: int32 [65536], P(('member', 'lon', 'lat')), parts along dimension 0, may hold values from 0 to 14
- obs_col: int32 [65536], P(('member', 'lon', 'lat')), parts along dimension 0, may hold values from 0 to 254
- obs_field: int32 [65536], P(('member', 'lon', 'lat')), parts along dimension 0, may hold values from 0 to 3
- obs_level: int32 [65536], P(('member', 'lon', 'lat')), parts along dimension 0, may hold values from 0 to 30
- land_mask: int32 [32, 2048], P('lat', 'lon'), may hold values 0 or 1
- kappa: float32 [32, 2048], P('lat', 'lon'), may hold values from 1 to 20
- sigma: float32 [128, 32, 2048], P(None, 'lat', 'lon'), may hold values from 0.5 to 2
- balance: float32 [128, 128], replicated, may hold values from -0.5 to 0.5
Outputs:
- gradient: float32 [256, 32, 2048], P('member', 'lat', 'lon'), parts along dimension 0
There are 2 independent parts, one for each index of `member`. A program takes and returns all parts, laid end to end along the dimension named above; an argument that names none is the same for every part. Nothing has to cross between parts.
Inputs may be any that keep to these rules, and one draw needn't show every extreme that they name: Within each device's block of 2048 innovations no tile is owner more than 256 times, and some tile is owner exactly 256 times.
All inputs are finite; a program needn't handle non-finite values. No bound on the sum of `land_mask` on one device may be relied on, other than what follows from the above.
Results may differ from a plain program's by a relative error of at most 0.0003.
Values sent between devices are 32-bit elements; how exact they have to be, the bound alone decides.
A program may use at most 64 MiB of HBM per device.

v0:
```python
import math

import jax
import jax.numpy as jnp
from jax import lax
from jax.sharding import PartitionSpec as P

LEV = 32


def with_halo(cells, sides, width):
    for axis, dim in sides:
        count = lax.axis_size(axis)
        ends = count - 1
        head = lax.slice_in_dim(cells, 0, width, axis=dim)
        tail = lax.slice_in_dim(cells, cells.shape[dim] - width, cells.shape[dim], axis=dim)
        cells = jnp.concatenate(
            [
                lax.ppermute(tail, axis, [(i, (i + 1) % count) for i in range(ends)]),
                cells,
                lax.ppermute(head, axis, [((i + 1) % count, i) for i in range(ends)]),
            ],
            axis=dim,
        )
    return cells


def corner_terms(values, fractions):
    fy = fractions[0]
    fx = fractions[1]
    fz = fractions[2]
    terms = []
    for lz in (0, 1):
        wz = fz if lz else 1.0 - fz
        for dy in (0, 1):
            wy = fy if dy else 1.0 - fy
            for dx in (0, 1):
                wx = fx if dx else 1.0 - fx
                terms.append(values * (wz * wy * wx))
    return jnp.stack(terms)


def face_coefficients(ext):
    kval = ext[0]
    mval = ext[1]
    kc = kval[1:-1, 1:-1]
    mc = mval[1:-1, 1:-1]
    south = 0.5 * (kc + kval[:-2, 1:-1]) * mc * mval[:-2, 1:-1]
    north = 0.5 * (kc + kval[2:, 1:-1]) * mc * mval[2:, 1:-1]
    west = 0.5 * (kc + kval[1:-1, :-2]) * mc * mval[1:-1, :-2]
    east = 0.5 * (kc + kval[1:-1, 2:]) * mc * mval[1:-1, 2:]
    denom = 1.0 + south + north + west + east
    return (south, north, west, east, denom)


def relax(u_ext, source, coefs):
    south, north, west, east, denom = coefs
    total = source + south * u_ext[:, :-2, 1:-1] + north * u_ext[:, 2:, 1:-1]
    total = total + west * u_ext[:, 1:-1, :-2] + east * u_ext[:, 1:-1, 2:]
    return total / denom


def bucket_rank(dest_hot):
    obs_dev, tiles = dest_hot.shape
    block_len = math.gcd(obs_dev, 512)
    nblocks = obs_dev // block_len
    hot_blocks = dest_hot.astype(jnp.bfloat16).reshape(nblocks, block_len, tiles)
    line = jnp.arange(block_len, dtype=jnp.int32)
    before = (line[:, None] > line[None, :]).astype(jnp.bfloat16)
    inside = jnp.einsum("ij,bjt->bit", before, hot_blocks, preferred_element_type=jnp.float32)
    block_totals = jnp.sum(dest_hot.reshape(nblocks, block_len, tiles), axis=1)
    block_start = jnp.cumsum(block_totals, axis=0) - block_totals
    placed = (inside + block_start[:, None, :]).reshape(obs_dev, tiles)
    return jnp.sum(placed * dest_hot, axis=1)


def grid_forcing(terms, received_base, chans, rows, cols):
    cells = rows * cols
    nitems = received_base.shape[0]
    block_len = math.gcd(nitems, 1024)
    nsteps = nitems // block_len
    chan_row = received_base // cells * rows + received_base % cells // cols
    column = received_base % cols
    term_blocks = jnp.transpose(terms.reshape(8, nsteps, block_len), (1, 0, 2))
    row_ids = jnp.arange(chans * rows, dtype=jnp.int32)[:, None]
    col_ids = jnp.arange(cols, dtype=jnp.int32)[None, :]

    def accumulate(total, pieces):
        term_blk, chan_blk, col_blk = pieces
        lefts = []
        rights = []
        for dx in (0, 1):
            left = jnp.zeros((chans * rows, block_len), jnp.float32)
            for lz in (0, 1):
                for dy in (0, 1):
                    target = chan_blk + lz * rows + dy
                    left = left + jnp.where(
                        row_ids == target[None, :], term_blk[lz * 4 + dy * 2 + dx][None, :], 0.0
                    )
            lefts.append(left)
            rights.append((col_blk[:, None] + dx == col_ids).astype(jnp.float32))
        update = jnp.dot(
            jnp.concatenate(lefts, axis=1),
            jnp.concatenate(rights, axis=0),
            precision=lax.Precision.HIGHEST,
            preferred_element_type=jnp.float32,
        )
        return (total + update, None)

    start = jnp.zeros((chans * rows, cols), jnp.float32)
    forcing, _ = lax.scan(
        accumulate,
        start,
        (term_blocks, chan_row.reshape(nsteps, block_len), column.reshape(nsteps, block_len)),
    )
    return forcing.reshape(chans, rows, cols)


def on_device(
    innovation,
    fractions,
    owner,
    obs_row,
    obs_col,
    obs_field,
    obs_level,
    land_mask,
    kappa,
    sigma,
    balance,
):
    n_lon = lax.axis_size("lon")
    n_lat = lax.axis_size("lat")
    tiles = n_lon * n_lat
    obs_dev = innovation.shape[0]
    slots = 2 * obs_dev // tiles
    chans, rows, cols = sigma.shape
    cells = rows * cols
    dest = owner[:, 0]
    tile_ids = jnp.arange(tiles, dtype=jnp.int32)
    dest_hot = (dest[:, None] == tile_ids[None, :]).astype(jnp.float32)
    rank = bucket_rank(dest_hot)
    slot_hot = (rank[:, None] == jnp.arange(slots, dtype=jnp.float32)[None, :]).astype(jnp.float32)
    channel = obs_field * LEV + obs_level
    base = channel * cells + obs_row * cols + obs_col
    payload = corner_terms(innovation, fractions)
    width = payload.shape[0]
    rows_all = jnp.concatenate([payload, base.astype(jnp.float32)[None, :]], axis=0)
    spread = rows_all[:, :, None] * dest_hot[None, :, :]
    placed = jnp.einsum(
        "wot,os->wts",
        spread,
        slot_hot,
        precision=lax.Precision.HIGHEST,
        preferred_element_type=jnp.float32,
    )
    float_buckets = placed[:width]
    int_buckets = placed[width:].astype(jnp.int32)
    got_float, got_int = (
        lax.all_to_all(float_buckets, ("lon", "lat"), split_axis=1, concat_axis=1, tiled=True),
        lax.all_to_all(int_buckets, ("lon", "lat"), split_axis=1, concat_axis=1, tiled=True),
    )
    received = got_float.reshape(width, -1)
    received_base = got_int.reshape(-1)
    maskf = land_mask.astype(jnp.float32)
    forcing = grid_forcing(received, received_base, chans, rows, cols) * maskf
    scaled = sigma * forcing
    balanced = jnp.dot(
        balance.T,
        scaled.reshape(chans, cells),
        precision=lax.Precision.HIGHEST,
        preferred_element_type=jnp.float32,
    ).reshape(chans, rows, cols)
    stacked = jnp.stack([kappa * maskf, maskf])
    ext = with_halo(stacked, (("lon", 2), ("lat", 1)), 1)
    coefs = face_coefficients(ext)
    field = balanced / coefs[4]
    for sweep in range(3):
        field_ext = with_halo(field, (("lon", 2), ("lat", 1)), 1)
        field = relax(field_ext, balanced, coefs)
    return field


def solution(mesh):
    in_specs = (
        P(("member", "lon", "lat")),
        P(None, ("member", "lon", "lat")),
        P(("member", "lon", "lat"), None),
        P(("member", "lon", "lat")),
        P(("member", "lon", "lat")),
        P(("member", "lon", "lat")),
        P(("member", "lon", "lat")),
        P("lat", "lon"),
        P("lat", "lon"),
        P(None, "lat", "lon"),
        P(),
    )
    out_specs = P("member", "lat", "lon")
    return jax.shard_map(
        on_device, mesh=mesh, in_specs=in_specs, out_specs=out_specs, check_vma=False
    )
```

profile of v0, /device:TPU:0, one launch (start us, length us, event | category | flops | bytes accessed | tf_op | source)
XLA Modules:
  0.0 206.1 jit_solution(1051553224901142849)
XLA Ops:
  1.6 4.8 %collective-permute-start = (f32[2,16,1]{2,1,0:T(8,128)S(1)}, f32[2,16,1]{2,1,0:T(8,128)S(1)}, u32[]{:S(2)}, u32[]{:S(2)}) collective-permute-start(f32[2,16,1]{2,1,0:T(8,128)S(1)} %get-tuple-element.198), channel_id=1, source_target_pairs={{0,2},{2,4},{4,6},{6,8},{8,10},{10,12},{12,14},{1,3},{3,5},{5,7},{... | collective-permute-start | bytes 392 | tf_op jit(solution)/shard_map/ppermute | solution.py:19
  9.1 1.4 reduce.5
  14.4 1.5 collective-permute-start.2
  17.8 7.6 %all-to-all-start = ((s32[1,16,256]{2,0,1:T(1,128)}), s32[1,16,256]{2,0,1:T(1,128)S(1)}, u32[]{:S(2)}, u32[]{:S(2)}) async-start(s32[1,16,256]{2,0,1:T(1,128)} %copy.52), calls=%async_computation | async-start | bytes 32768 | tf_op jit(solution)/shard_map/all_to_all | solution.py:161
  26.3 5.6 %all-to-all-done = s32[1,16,256]{2,0,1:T(1,128)S(1)} async-done(((s32[1,16,256]{2,0,1:T(1,128)}), s32[1,16,256]{2,0,1:T(1,128)S(1)}, u32[]{:S(2)}, u32[]{:S(2)}) %all-to-all-start) | async-done | bytes 16416 | tf_op jit(solution)/shard_map/all_to_all | solution.py:161
  32.0 3.5 %all-to-all-start.1 = ((f32[8,16,256]{2,0,1:T(8,128)}), f32[8,16,256]{2,0,1:T(8,128)S(1)}, u32[]{:S(2)}, u32[]{:S(2)}) async-start(f32[8,16,256]{2,0,1:T(8,128)} %copy.53), calls=%async_computation.1 | async-start | bytes 262144 | tf_op jit(solution)/shard_map/all_to_all | solution.py:160
  35.8 7.6 %all-to-all-done.1 = f32[8,16,256]{2,0,1:T(8,128)S(1)} async-done(((f32[8,16,256]{2,0,1:T(8,128)}), f32[8,16,256]{2,0,1:T(8,128)S(1)}, u32[]{:S(2)}, u32[]{:S(2)}) %all-to-all-start.1) | async-done | bytes 131104 | tf_op jit(solution)/shard_map/all_to_all | solution.py:160
  43.4 90.1 %while.14 = (s32[]{:T(128)}, f32[2048,256]{1,0:T(8,128)}, s32[4,1024]{1,0:T(4,128)S(1)}, f32[4,8,1024]{2,1,0:T(8,128)S(1)}, s32[4,1024]{1,0:T(4,128)S(1)}, /*ind...) while((s32[]{:T(128)}, f32[2048,256]{1,0:T(8,128)}, ...), condition=%wide.region_4.5_spmd.clone.clone, body=%wide.region_3.4_spmd.clone.clone.sunk | while | flops 12928946176 | bytes 38961412 | solution.py:111
  43.4 9.5 %fusion.98 = (f32[2048,1024]{1,0:T(8,128)}, f32[2048,1024]{1,0:T(8,128)}) fusion(f32[1024]{0:T(1024)S(1)} %bitcast.101, s32[1024]{0:T(1024)S(1)} %bitcast.106, f32[1024]{0:T(1024)S(1)} %bitcast.102, s32[1024]{0:T(1024)S(1)} %bitcast.105, f32[1024]{0:T(1024)S(1)} %bitcast.103, s32[1024]{0:T(1024)S(1)} %bitcast.107, f32[1024]{0:T(1024)S(1)} %bitcast.97, ...), kind=kLoop, calls=%fused_computation.18.clone.1 | loop fusion | flops 37748736 | bytes 16826368 | tf_op jit(solution)/shard_map/while/body/eval_jaxpr/add | solution.py:97
  53.3 12.4 %fusion.99 = f32[2048,256]{1,0:T(8,128)} fusion(f32[2048,1024]{1,0:T(8,128)} %get-tuple-element.273, f32[2048,1024]{1,0:T(8,128)} %get-tuple-element.274, f32[2048,256]{1,0:T(8,128)} %get-tuple-element.291, pred[1024,256]{1,0:T(32,128)(4,1)S(1)} %iota_compare_fusion.12, pred[1024,256]{1,0:T(32,128)(4,1)S(1)} %iota_compare_fusion.13, pred[]{:T(512)S(6)} %compare.13), kind=kOutput, calls=%fused_computation.24.clone.1 | convolution fusion | flops 12890669056 | bytes 21495808 | tf_op jit(solution)/shard_map/while/body/eval_jaxpr/dot_general | solution.py:102
  65.8 9.5 %fusion.98 = (f32[2048,1024]{1,0:T(8,128)}, f32[2048,1024]{1,0:T(8,128)}) fusion(f32[1024]{0:T(1024)S(1)} %bitcast.101, s32[1024]{0:T(1024)S(1)} %bitcast.106, f32[1024]{0:T(1024)S(1)} %bitcast.102, s32[1024]{0:T(1024)S(1)} %bitcast.105, f32[1024]{0:T(1024)S(1)} %bitcast.103, s32[1024]{0:T(1024)S(1)} %bitcast.107, f32[1024]{0:T(1024)S(1)} %bitcast.97, ...), kind=kLoop, calls=%fused_computation.18.clone.1 | loop fusion | flops 37748736 | bytes 16826368 | tf_op jit(solution)/shard_map/while/body/eval_jaxpr/add | solution.py:97
  75.7 12.6 %fusion.99 = f32[2048,256]{1,0:T(8,128)} fusion(f32[2048,1024]{1,0:T(8,128)} %get-tuple-element.273, f32[2048,1024]{1,0:T(8,128)} %get-tuple-element.274, f32[2048,256]{1,0:T(8,128)} %get-tuple-element.291, pred[1024,256]{1,0:T(32,128)(4,1)S(1)} %iota_compare_fusion.12, pred[1024,256]{1,0:T(32,128)(4,1)S(1)} %iota_compare_fusion.13, pred[]{:T(512)S(6)} %compare.13), kind=kOutput, calls=%fused_computation.24.clone.1 | convolution fusion | flops 12890669056 | bytes 21495808 | tf_op jit(solution)/shard_map/while/body/eval_jaxpr/dot_general | solution.py:102
  88.4 9.5 %fusion.98 = (f32[2048,1024]{1,0:T(8,128)}, f32[2048,1024]{1,0:T(8,128)}) fusion(f32[1024]{0:T(1024)S(1)} %bitcast.101, s32[1024]{0:T(1024)S(1)} %bitcast.106, f32[1024]{0:T(1024)S(1)} %bitcast.102, s32[1024]{0:T(1024)S(1)} %bitcast.105, f32[1024]{0:T(1024)S(1)} %bitcast.103, s32[1024]{0:T(1024)S(1)} %bitcast.107, f32[1024]{0:T(1024)S(1)} %bitcast.97, ...), kind=kLoop, calls=%fused_computation.18.clone.1 | loop fusion | flops 37748736 | bytes 16826368 | tf_op jit(solution)/shard_map/while/body/eval_jaxpr/add | solution.py:97
  98.3 12.6 %fusion.99 = f32[2048,256]{1,0:T(8,128)} fusion(f32[2048,1024]{1,0:T(8,128)} %get-tuple-element.273, f32[2048,1024]{1,0:T(8,128)} %get-tuple-element.274, f32[2048,256]{1,0:T(8,128)} %get-tuple-element.291, pred[1024,256]{1,0:T(32,128)(4,1)S(1)} %iota_compare_fusion.12, pred[1024,256]{1,0:T(32,128)(4,1)S(1)} %iota_compare_fusion.13, pred[]{:T(512)S(6)} %compare.13), kind=kOutput, calls=%fused_computation.24.clone.1 | convolution fusion | flops 12890669056 | bytes 21495808 | tf_op jit(solution)/shard_map/while/body/eval_jaxpr/dot_general | solution.py:102
  110.9 9.5 %fusion.98 = (f32[2048,1024]{1,0:T(8,128)}, f32[2048,1024]{1,0:T(8,128)}) fusion(f32[1024]{0:T(1024)S(1)} %bitcast.101, s32[1024]{0:T(1024)S(1)} %bitcast.106, f32[1024]{0:T(1024)S(1)} %bitcast.102, s32[1024]{0:T(1024)S(1)} %bitcast.105, f32[1024]{0:T(1024)S(1)} %bitcast.103, s32[1024]{0:T(1024)S(1)} %bitcast.107, f32[1024]{0:T(1024)S(1)} %bitcast.97, ...), kind=kLoop, calls=%fused_computation.18.clone.1 | loop fusion | flops 37748736 | bytes 16826368 | tf_op jit(solution)/shard_map/while/body/eval_jaxpr/add | solution.py:97
  120.8 12.6 %fusion.99 = f32[2048,256]{1,0:T(8,128)} fusion(f32[2048,1024]{1,0:T(8,128)} %get-tuple-element.273, f32[2048,1024]{1,0:T(8,128)} %get-tuple-element.274, f32[2048,256]{1,0:T(8,128)} %get-tuple-element.291, pred[1024,256]{1,0:T(32,128)(4,1)S(1)} %iota_compare_fusion.12, pred[1024,256]{1,0:T(32,128)(4,1)S(1)} %iota_compare_fusion.13, pred[]{:T(512)S(6)} %compare.13), kind=kOutput, calls=%fused_computation.24.clone.1 | convolution fusion | flops 12890669056 | bytes 21495808 | tf_op jit(solution)/shard_map/while/body/eval_jaxpr/dot_general | solution.py:102
  133.4 2.7 %multiply_multiply_fusion = f32[128,16,256]{2,1,0:T(8,128)S(1)} fusion(f32[128,16,256]{2,1,0:T(8,128)} %param.22, f32[128,16,256]{2,1,0:T(8,128)} %bitcast.92, f32[16,256]{1,0:T(8,128)S(1)} %get-tuple-element.212), kind=kLoop, calls=%fused_computation.97 | loop fusion | flops 1048576 | bytes 6307840 | tf_op jit(solution)/shard_map/mul | solution.py:167
  136.1 1.6 copy.77
  137.8 3.5 %fusion.89 = f32[4096,128]{1,0:T(8,128)S(1)} fusion(f32[128,4096]{1,0:T(8,128)S(1)} %bitcast.91, f32[128,128]{1,0:T(8,128)S(1)} %copy-done), kind=kOutput, calls=%fused_computation.192 | convolution fusion | flops 805306368 | bytes 4259840 | tf_op jit(solution)/shard_map/dot_general | solution.py:168
  141.3 1.3 copy_divide_fusion
  145.3 4.2 %collective-permute-done.5 = f32[128,16,1]{0,1,2:T(8,128)S(1)} collective-permute-done((f32[128,16,1]{0,1,2:T(8,128)S(1)}, f32[128,16,1]{0,1,2:T(8,128)S(1)}, u32[]{:S(2)}, u32[]{:S(2)}) %collective-permute-start.5) | collective-permute-done | bytes 8224 | tf_op jit(solution)/shard_map/ppermute | solution.py:21
  152.9 1.4 collective-permute-done.7
  154.4 9.0 %fusion.50 = f32[128,16,256]{0,1,2:T(8,128)S(1)} fusion(f32[128,16,1]{0,1,2:T(8,128)S(1)} %collective-permute-done.5, f32[128,16,256]{0,1,2:T(8,128)} %copy-done.1, f32[128,16,1]{0,1,2:T(8,128)S(1)} %collective-permute-done.4, f32[128,1,258]{0,1,2:T(1,128)S(1)} %copy.62, f32[128,1,258]{0,1,2:T(1,128)S(1)} %copy.58, f32[128,16,256]{0,2,1:T(8,128)S(1)} %bitcast.87, ...), kind=kLoop, calls=%fused_computation.83 | loop fusion | flops 8912896 | bytes 6653952 | tf_op jit(solution)/shard_map/div | solution.py:60
  163.5 4.3 %collective-permute-start.8 = (f32[128,16,1]{0,1,2:T(8,128)S(1)}, f32[128,16,1]{0,1,2:T(8,128)S(1)}, u32[]{:S(2)}, u32[]{:S(2)}) collective-permute-start(f32[128,16,1]{0,1,2:T(8,128)S(1)} %get-tuple-element.190), channel_id=1, source_target_pairs={{0,2},{2,4},{4,6},{6,8},{8,10},{10,12},{12,14},{1,3},{3,5},{5,7},{... | collective-permute-start | bytes 24584 | tf_op jit(solution)/shard_map/ppermute | solution.py:19
  169.1 4.2 %collective-permute-done.9 = f32[128,16,1]{0,1,2:T(8,128)S(1)} collective-permute-done((f32[128,16,1]{0,1,2:T(8,128)S(1)}, f32[128,16,1]{0,1,2:T(8,128)S(1)}, u32[]{:S(2)}, u32[]{:S(2)}) %collective-permute-start.9) | collective-permute-done | bytes 8224 | tf_op jit(solution)/shard_map/ppermute | solution.py:21
  176.3 1.8 collective-permute-done.11
  178.2 5.3 %fusion.41 = f32[128,16,256]{0,1,2:T(8,128)S(1)} fusion(f32[128,16,1]{0,1,2:T(8,128)S(1)} %collective-permute-done.9, f32[128,16,256]{0,1,2:T(8,128)S(1)} %fusion.50, f32[128,16,1]{0,1,2:T(8,128)S(1)} %collective-permute-done.8, f32[128,1,258]{0,1,2:T(1,128)S(1)} %copy.69, f32[128,1,258]{0,1,2:T(1,128)S(1)} %copy.66, f32[128,16,256]{0,2,1:T(8,128)S(1)} %bitcast.88, ...), kind=kLoop, calls=%fused_computation.66 | loop fusion | flops 8912896 | bytes 6653952 | tf_op jit(solution)/shard_map/div | solution.py:60
  183.6 2.8 %collective-permute-start.12 = (f32[128,16,1]{0,1,2:T(8,128)S(1)}, f32[128,16,1]{0,1,2:T(8,128)S(1)}, u32[]{:S(2)}, u32[]{:S(2)}) collective-permute-start(f32[128,16,1]{0,1,2:T(8,128)S(1)} %get-tuple-element.188), channel_id=1, source_target_pairs={{0,2},{2,4},{4,6},{6,8},{8,10},{10,12},{12,14},{1,3},{3,5},{5,7},{... | collective-permute-start | bytes 24584 | tf_op jit(solution)/shard_map/ppermute | solution.py:19
  187.8 4.2 %collective-permute-done.13 = f32[128,16,1]{0,1,2:T(8,128)S(1)} collective-permute-done((f32[128,16,1]{0,1,2:T(8,128)S(1)}, f32[128,16,1]{0,1,2:T(8,128)S(1)}, u32[]{:S(2)}, u32[]{:S(2)}) %collective-permute-start.13) | collective-permute-done | bytes 8224 | tf_op jit(solution)/shard_map/ppermute | solution.py:21
  194.9 1.8 collective-permute-done.15
  196.9 6.1 %fusion.32 = f32[128,16,256]{0,1,2:T(8,128)} fusion(f32[128,16,1]{0,1,2:T(8,128)S(1)} %collective-permute-done.13, f32[128,16,256]{0,1,2:T(8,128)S(1)} %fusion.41, f32[128,16,1]{0,1,2:T(8,128)S(1)} %collective-permute-done.12, f32[128,1,258]{0,1,2:T(1,128)S(1)} %copy.74, f32[128,1,258]{0,1,2:T(1,128)S(1)} %copy.71, f32[128,16,256]{0,2,1:T(8,128)S(1)} %bitcast.89, ...), kind=kLoop, calls=%fused_computation.49 | loop fusion | flops 8912896 | bytes 6653952 | tf_op jit(solution)/shard_map/div | solution.py:60
  203.0 3.1 %copy.75 = f32[128,16,256]{2,1,0:T(8,128)} copy(f32[128,16,256]{0,1,2:T(8,128)} %fusion.32) | data formatting | bytes 4194304 | tf_op jit(solution)/shard_map/div | solution.py:60
  (101 shorter events, 28.1 us)
Async XLA Ops:
  0.0 137.8 %copy-start = (f32[128,128]{1,0:T(8,128)S(1)}, f32[128,128]{1,0:T(8,128)}, u32[]{:S(2)}) copy-start(f32[128,128]{1,0:T(8,128)} %param.23) | copy-start | bytes 196612
  1.6 12.8 %collective-permute-start = (f32[2,16,1]{2,1,0:T(8,128)S(1)}, f32[2,16,1]{2,1,0:T(8,128)S(1)}, u32[]{:S(2)}, u32[]{:S(2)}) collective-permute-start(f32[2,16,1]{2,1,0:T(8,128)S(1)} %get-tuple-element.198), channel_id=1, source_target_pairs={{0,2},{2,4},{4,6},{6,8},{8,10},{10,12},{12,14},{1,3},{3,5},{5,7},{... | collective-permute-start | bytes 392 | tf_op jit(solution)/shard_map/ppermute | solution.py:19
  6.4 7.9 %collective-permute-start.1 = (f32[2,16,1]{2,1,0:T(8,128)S(1)}, f32[2,16,1]{2,1,0:T(8,128)S(1)}, u32[]{:S(2)}, u32[]{:S(2)}) collective-permute-start(f32[2,16,1]{2,1,0:T(8,128)S(1)} %get-tuple-element.199), channel_id=1, source_target_pairs={{2,0},{4,2},{6,4},{8,6},{10,8},{12,10},{14,12},{3,1},{5,3},{7,5},{... | collective-permute-start | bytes 392 | tf_op jit(solution)/shard_map/ppermute | solution.py:21
  14.4 11.8 %collective-permute-start.2 = (f32[2,1,258]{2,1,0:T(1,128)S(1)}, f32[2,1,258]{2,1,0:T(1,128)S(1)}, u32[]{:S(2)}, u32[]{:S(2)}) collective-permute-start(f32[2,1,258]{2,1,0:T(1,128)S(1)} %get-tuple-element.196), channel_id=1, source_target_pairs={{0,1},{2,3},{4,5},{6,7},{8,9},{10,11},{12,13},{14,15},{16,17},{18,... | collective-permute-start | bytes 6200 | tf_op jit(solution)/shard_map/ppermute | solution.py:19
  15.9 10.3 %collective-permute-start.3 = (f32[2,1,258]{2,1,0:T(1,128)S(1)}, f32[2,1,258]{2,1,0:T(1,128)S(1)}, u32[]{:S(2)}, u32[]{:S(2)}) collective-permute-start(f32[2,1,258]{2,1,0:T(1,128)S(1)} %get-tuple-element.197), channel_id=1, source_target_pairs={{1,0},{3,2},{5,4},{7,6},{9,8},{11,10},{13,12},{15,14},{17,16},{19,... | collective-permute-start | bytes 6200 | tf_op jit(solution)/shard_map/ppermute | solution.py:21
  17.8 14.1 %all-to-all-start = ((s32[1,16,256]{2,0,1:T(1,128)}), s32[1,16,256]{2,0,1:T(1,128)S(1)}, u32[]{:S(2)}, u32[]{:S(2)}) async-start(s32[1,16,256]{2,0,1:T(1,128)} %copy.52), calls=%async_computation | async-start | bytes 32768 | tf_op jit(solution)/shard_map/all_to_all | solution.py:161
  32.0 11.4 %all-to-all-start.1 = ((f32[8,16,256]{2,0,1:T(8,128)}), f32[8,16,256]{2,0,1:T(8,128)S(1)}, u32[]{:S(2)}, u32[]{:S(2)}) async-start(f32[8,16,256]{2,0,1:T(8,128)} %copy.53), calls=%async_computation.1 | async-start | bytes 262144 | tf_op jit(solution)/shard_map/all_to_all | solution.py:160
  142.7 6.9 %copy-start.1 = (f32[128,16,256]{0,1,2:T(8,128)}, f32[128,16,256]{0,1,2:T(8,128)S(1)}, u32[]{:S(2)}) copy-start(f32[128,16,256]{0,1,2:T(8,128)S(1)} %copy_divide_fusion) | copy-start | bytes 6291460
  142.7 2.6 %collective-permute-start.4 = (f32[128,16,1]{0,1,2:T(8,128)S(1)}, f32[128,16,1]{0,1,2:T(8,128)S(1)}, u32[]{:S(2)}, u32[]{:S(2)}) collective-permute-start(f32[128,16,1]{0,1,2:T(8,128)S(1)} %get-tuple-element.192), channel_id=1, source_target_pairs={{0,2},{2,4},{4,6},{6,8},{8,10},{10,12},{12,14},{1,3},{3,5},{5,7},{... | collective-permute-start | bytes 24584 | tf_op jit(solution)/shard_map/ppermute | solution.py:19
  144.0 5.5 %collective-permute-start.5 = (f32[128,16,1]{0,1,2:T(8,128)S(1)}, f32[128,16,1]{0,1,2:T(8,128)S(1)}, u32[]{:S(2)}, u32[]{:S(2)}) collective-permute-start(f32[128,16,1]{0,1,2:T(8,128)S(1)} %get-tuple-element.193), channel_id=1, source_target_pairs={{2,0},{4,2},{6,4},{8,6},{10,8},{12,10},{14,12},{3,1},{5,3},{7,5},{... | collective-permute-start | bytes 24584 | tf_op jit(solution)/shard_map/ppermute | solution.py:21
  149.7 3.0 %collective-permute-start.6 = (f32[128,1,258]{0,2,1:T(8,128)S(1)}, f32[128,1,258]{0,2,1:T(8,128)S(1)}, u32[]{:S(2)}, u32[]{:S(2)}) collective-permute-start(f32[128,1,258]{0,2,1:T(8,128)S(1)} %copy.57), channel_id=1, source_target_pairs={{0,1},{2,3},{4,5},{6,7},{8,9},{10,11},{12,13},{14,15},{16,17},{18,... | collective-permute-start | bytes 396296 | tf_op jit(solution)/shard_map/ppermute | solution.py:19
  151.1 3.2 %collective-permute-start.7 = (f32[128,1,258]{0,2,1:T(8,128)S(1)}, f32[128,1,258]{0,2,1:T(8,128)S(1)}, u32[]{:S(2)}, u32[]{:S(2)}) collective-permute-start(f32[128,1,258]{0,2,1:T(8,128)S(1)} %copy.61), channel_id=1, source_target_pairs={{1,0},{3,2},{5,4},{7,6},{9,8},{11,10},{13,12},{15,14},{17,16},{19,... | collective-permute-start | bytes 396296 | tf_op jit(solution)/shard_map/ppermute | solution.py:21
  163.5 5.6 %collective-permute-start.8 = (f32[128,16,1]{0,1,2:T(8,128)S(1)}, f32[128,16,1]{0,1,2:T(8,128)S(1)}, u32[]{:S(2)}, u32[]{:S(2)}) collective-permute-start(f32[128,16,1]{0,1,2:T(8,128)S(1)} %get-tuple-element.190), channel_id=1, source_target_pairs={{0,2},{2,4},{4,6},{6,8},{8,10},{10,12},{12,14},{1,3},{3,5},{5,7},{... | collective-permute-start | bytes 24584 | tf_op jit(solution)/shard_map/ppermute | solution.py:19
  167.8 5.5 %collective-permute-start.9 = (f32[128,16,1]{0,1,2:T(8,128)S(1)}, f32[128,16,1]{0,1,2:T(8,128)S(1)}, u32[]{:S(2)}, u32[]{:S(2)}) collective-permute-start(f32[128,16,1]{0,1,2:T(8,128)S(1)} %get-tuple-element.191), channel_id=1, source_target_pairs={{2,0},{4,2},{6,4},{8,6},{10,8},{12,10},{14,12},{3,1},{5,3},{7,5},{... | collective-permute-start | bytes 24584 | tf_op jit(solution)/shard_map/ppermute | solution.py:21
  173.5 2.6 %collective-permute-start.10 = (f32[128,1,258]{0,2,1:T(8,128)S(1)}, f32[128,1,258]{0,2,1:T(8,128)S(1)}, u32[]{:S(2)}, u32[]{:S(2)}) collective-permute-start(f32[128,1,258]{0,2,1:T(8,128)S(1)} %copy.65), channel_id=1, source_target_pairs={{0,1},{2,3},{4,5},{6,7},{8,9},{10,11},{12,13},{14,15},{16,17},{18,... | collective-permute-start | bytes 396296 | tf_op jit(solution)/shard_map/ppermute | solution.py:19
  174.8 3.2 %collective-permute-start.11 = (f32[128,1,258]{0,2,1:T(8,128)S(1)}, f32[128,1,258]{0,2,1:T(8,128)S(1)}, u32[]{:S(2)}, u32[]{:S(2)}) collective-permute-start(f32[128,1,258]{0,2,1:T(8,128)S(1)} %copy.68), channel_id=1, source_target_pairs={{1,0},{3,2},{5,4},{7,6},{9,8},{11,10},{13,12},{15,14},{17,16},{19,... | collective-permute-start | bytes 396296 | tf_op jit(solution)/shard_map/ppermute | solution.py:21
  183.6 4.2 %collective-permute-start.12 = (f32[128,16,1]{0,1,2:T(8,128)S(1)}, f32[128,16,1]{0,1,2:T(8,128)S(1)}, u32[]{:S(2)}, u32[]{:S(2)}) collective-permute-start(f32[128,16,1]{0,1,2:T(8,128)S(1)} %get-tuple-element.188), channel_id=1, source_target_pairs={{0,2},{2,4},{4,6},{6,8},{8,10},{10,12},{12,14},{1,3},{3,5},{5,7},{... | collective-permute-start | bytes 24584 | tf_op jit(solution)/shard_map/ppermute | solution.py:19
  186.4 5.5 %collective-permute-start.13 = (f32[128,16,1]{0,1,2:T(8,128)S(1)}, f32[128,16,1]{0,1,2:T(8,128)S(1)}, u32[]{:S(2)}, u32[]{:S(2)}) collective-permute-start(f32[128,16,1]{0,1,2:T(8,128)S(1)} %get-tuple-element.189), channel_id=1, source_target_pairs={{2,0},{4,2},{6,4},{8,6},{10,8},{12,10},{14,12},{3,1},{5,3},{7,5},{... | collective-permute-start | bytes 24584 | tf_op jit(solution)/shard_map/ppermute | solution.py:21
  192.2 2.6 %collective-permute-start.14 = (f32[128,1,258]{0,2,1:T(8,128)S(1)}, f32[128,1,258]{0,2,1:T(8,128)S(1)}, u32[]{:S(2)}, u32[]{:S(2)}) collective-permute-start(f32[128,1,258]{0,2,1:T(8,128)S(1)} %copy.70), channel_id=1, source_target_pairs={{0,1},{2,3},{4,5},{6,7},{8,9},{10,11},{12,13},{14,15},{16,17},{18,... | collective-permute-start | bytes 396296 | tf_op jit(solution)/shard_map/ppermute | solution.py:19
  193.5 3.2 %collective-permute-start.15 = (f32[128,1,258]{0,2,1:T(8,128)S(1)}, f32[128,1,258]{0,2,1:T(8,128)S(1)}, u32[]{:S(2)}, u32[]{:S(2)}) collective-permute-start(f32[128,1,258]{0,2,1:T(8,128)S(1)} %copy.73), channel_id=1, source_target_pairs={{1,0},{3,2},{5,4},{7,6},{9,8},{11,10},{13,12},{15,14},{17,16},{19,... | collective-permute-start | bytes 396296 | tf_op jit(solution)/shard_map/ppermute | solution.py:21
where the time goes:
time: 207 us; the launch traced here: 206 us
  other arithmetic  70.3 us (34%)
  matrix products  55 us (27%)
  starting transfers between devices  40.1 us (19%)
  waiting for transfers between devices  30.9 us (15%)
  local copies, waits for them, and re-layouts  9.2 us (4%)
    dot_general x4, matrix products, accumulate(): jnp.dot(jnp.concatenate(lefts, axis=1), jnp.concatenate(rights, axis=0),...  50.1 us
    add x4, other arithmetic, accumulate(): left + jnp.where(row_ids == target[None, :], term_blk[lz * 4 + dy * 2 + d...  37.8 us
    div x3, other arithmetic, relax(): return total / denom  20.4 us
    ppermute x8, starting transfers between devices, with_halo(): lax.ppermute(tail, axis, [(i, (i + 1) % count) for i in range(ends)])  18.6 us
    ppermute x8, waiting for transfers between devices, with_halo(): lax.ppermute(head, axis, [((i + 1) % count, i) for i in range(ends)])  17.6 us
    ppermute x8, starting transfers between devices, with_halo(): lax.ppermute(head, axis, [((i + 1) % count, i) for i in range(ends)])  10.3 us
    all_to_all x1, starting transfers between devices, on_device(): lax.all_to_all(int_buckets, ('lon', 'lat'), split_axis=1, concat_axis=1,...  7.62 us
    all_to_all x1, waiting for transfers between devices, on_device(): lax.all_to_all(float_buckets, ('lon', 'lat'), split_axis=1, concat_axis=1...  7.55 us
  transfers between devices with their start and end apart: 18, of which 8 were waited for; matrix products, arithmetic and copies ran while one was open for 4% of the time, Pallas kernels for 0%

commit v1 on v0

v1 whole, which is shorter than its diff:
```python
import functools
import math

import jax
import jax.numpy as jnp
from jax import lax
from jax.experimental import pallas as pl
from jax.experimental.pallas import tpu as pltpu
from jax.sharding import PartitionSpec as P

LEV = 32
MESH = pl.DeviceIdType.MESH
NT = (((1,), (1,)), ((), ()))
LANES = 128


def iota_f(shape, dim):
    return lax.broadcasted_iota(jnp.int32, shape, dim).astype(jnp.float32)


def hat(ids, low, first, second):
    return jnp.where(ids == low, first, 0.0) + jnp.where(ids == low + 1.0, second, 0.0)


def split2(x):
    hi = x.astype(jnp.bfloat16)
    return hi, (x - hi.astype(jnp.float32)).astype(jnp.bfloat16)


def buckets(innov, frac, owner, orow, ocol, ofield, olev, tiles, slots):
    obs = innov.shape[1]
    blk = math.gcd(obs, 256)
    dest = owner[...]
    hot = jnp.where(lax.broadcasted_iota(jnp.int32, (tiles, obs), 0) == dest, 1.0, 0.0)
    before = jnp.where(iota_f((blk, blk), 0) < iota_f((blk, blk), 1), 1.0, 0.0).astype(jnp.bfloat16)
    carry = jnp.zeros((tiles, 1), jnp.float32)
    ranks = []
    for b in range(obs // blk):
        part = hot[:, b * blk : (b + 1) * blk]
        ahead = jnp.dot(part.astype(jnp.bfloat16), before, preferred_element_type=jnp.float32) + carry
        ranks.append(jnp.sum(ahead * part, axis=0, keepdims=True))
        carry = carry + jnp.sum(part, axis=1, keepdims=True)
    rank = jnp.concatenate(ranks, axis=1)
    slot_hot = jnp.where(iota_f((slots, obs), 0) == rank, 1.0, 0.0).astype(jnp.bfloat16)
    channel = ofield[...] * LEV + olev[...]
    ints = [channel.astype(jnp.float32), orow[...].astype(jnp.float32), ocol[...].astype(jnp.float32)]
    rest = jnp.concatenate(
        [innov[...], frac[...]] + ints + [jnp.zeros((1, obs), jnp.float32)], axis=0
    )
    mine = lax.broadcasted_iota(jnp.int32, (tiles, 8, obs), 0) == dest[None]
    placed = jnp.zeros((tiles * 8, slots), jnp.float32)
    for piece in range(3):
        top = rest.astype(jnp.bfloat16).astype(jnp.float32)
        rest = rest - top
        spread = jnp.where(mine, top[None], 0.0).reshape(tiles * 8, obs).astype(jnp.bfloat16)
        placed = placed + lax.dot_general(spread, slot_hot, NT, preferred_element_type=jnp.float32)
    return placed.reshape(tiles, 8, slots)


def kernel(
    n_lon,
    n_lat,
    innov,
    frac,
    owner,
    orow,
    ocol,
    ofield,
    olev,
    mask,
    kappa,
    balance,
    sigma,
    out,
    sig,
    send,
    recv,
    km,
    km_in,
    coef,
    a_ref,
    b_ref,
    r_hi,
    r_lo,
    acc,
    u,
    edge_out,
    edge_in,
    edge_t,
    packs,
    sig_sem,
    send_sem,
    recv_sem,
    km_send,
    km_recv,
    halo_send,
    halo_recv,
):
    tiles = n_lon * n_lat
    rows, cols = mask.shape
    chans = balance.shape[0]
    slots = recv.shape[2]
    halves = cols // LANES
    lon = lax.axis_index("lon")
    lat = lax.axis_index("lat")
    me = lon * n_lat + lat

    def where_is(tile):
        return {"lon": tile // n_lat, "lat": lax.rem(tile, n_lat)}

    sig_copy = pltpu.make_async_copy(sigma, sig, sig_sem)
    sig_copy.start()
    barrier = pltpu.get_barrier_semaphore()

    @pl.loop(1, tiles)
    def _(k):
        pl.semaphore_signal(
            barrier, inc=1, device_id=where_is(lax.rem(me + k, tiles)), device_id_type=MESH
        )

    maskf = mask[...].astype(jnp.float32)
    km[0] = kappa[...] * maskf
    km[1] = maskf
    send[...] = buckets(innov, frac, owner, orow, ocol, ofield, olev, tiles, slots)
    pl.semaphore_wait(barrier, tiles - 1)

    def item_copy(target, origin):
        return pltpu.make_async_remote_copy(
            src_ref=send.at[target],
            dst_ref=recv.at[origin],
            send_sem=send_sem.at[target],
            recv_sem=recv_sem.at[origin],
            device_id=where_is(target),
            device_id_type=MESH,
        )

    @pl.loop(1, tiles)
    def _(k):
        item_copy(lax.rem(me + k, tiles), me).start()

    has = (lat > 0, lat < n_lat - 1, lon > 0, lon < n_lon - 1)
    there = (
        {"lat": lat - 1},
        {"lat": lat + 1},
        {"lon": lon - 1},
        {"lon": lon + 1},
    )
    opposite = (1, 0, 3, 2)

    def km_copy(side):
        return pltpu.make_async_remote_copy(
            src_ref=km,
            dst_ref=km_in.at[opposite[side]],
            send_sem=km_send.at[side],
            recv_sem=km_recv.at[opposite[side]],
            device_id=there[side],
            device_id_type=MESH,
        )

    def km_arrival(side):
        return pltpu.make_async_remote_copy(
            src_ref=km,
            dst_ref=km_in.at[side],
            send_sem=km_send.at[side],
            recv_sem=km_recv.at[side],
            device_id=there[side],
            device_id_type=MESH,
        )

    for side in range(4):

        @pl.when(has[side])
        def _():
            km_copy(side).start()

        @pl.when(jnp.logical_not(has[side]))
        def _():
            km_in[side] = jnp.zeros((2, rows, cols), jnp.float32)

    recv[me] = send[me]
    acc[...] = jnp.zeros(acc.shape, jnp.float32)
    group = a_ref.shape[1] // slots
    step_rows = math.gcd(rows, 4)

    @pl.loop(0, tiles // group)
    def _(chunk):
        pieces = []
        for i in range(group):
            k = chunk * group + i
            origin = lax.rem(me + tiles - k, tiles)

            @pl.when(k > 0)
            def _():
                item_copy(origin, origin).wait_recv()

            pieces.append(recv[origin])
        items = pieces[0] if group == 1 else jnp.concatenate(pieces, axis=1)
        depth = items.shape[1]
        val, fy, fx, fz = items[0:1], items[1:2], items[2:3], items[3:4]
        ch, row, col = items[4:5], items[5:6], items[6:7]
        a_ref[...] = hat(iota_f((chans, depth), 0), ch, val * (1.0 - fz), val * fz)
        b_ref[...] = hat(iota_f((rows, depth), 0), row, 1.0 - fy, fy)
        hi, lo = split2(hat(iota_f((cols, depth), 0), col, 1.0 - fx, fx))
        r_hi[...] = hi
        r_lo[...] = lo

        @pl.loop(0, rows // step_rows)
        def _(part):
            lefts = [
                a_ref[...] * b_ref[pl.ds(part * step_rows + j, 1), :] for j in range(step_rows)
            ]
            left_hi, left_lo = split2(jnp.concatenate(lefts, axis=0))
            dot = functools.partial(
                lax.dot_general, dimension_numbers=NT, preferred_element_type=jnp.float32
            )
            total = dot(left_hi, r_hi[...]) + dot(left_lo, r_hi[...]) + dot(left_hi, r_lo[...])
            here = pl.ds(pl.multiple_of(part * step_rows, step_rows), step_rows)
            acc[here] += total.reshape(step_rows, chans, cols)

    for side in range(4):

        @pl.when(has[side])
        def _():
            km_arrival(side).wait_recv()
            km_copy(side).wait_send()

    kc, mc = km[0], km[1]

    def beside(plane):
        mid = km[plane]
        south = jnp.concatenate([km_in[0, plane][rows - 1 :], mid[: rows - 1]], axis=0)
        north = jnp.concatenate([mid[1:], km_in[1, plane][:1]], axis=0)
        west = jnp.concatenate([km_in[2, plane][:, cols - 1 :], mid[:, : cols - 1]], axis=1)
        east = jnp.concatenate([mid[:, 1:], km_in[3, plane][:, :1]], axis=1)
        return (south, north, west, east)

    faces = [0.5 * (kc + kn) * mc * mn for kn, mn in zip(beside(0), beside(1))]
    inv = 1.0 / (1.0 + faces[0] + faces[1] + faces[2] + faces[3])
    for side in range(4):
        coef[side] = faces[side] * inv
    coef[4] = inv
    coef[5] = mc

    lane = lax.broadcasted_iota(jnp.int32, (chans, LANES), 1)

    def pack(r, first, last):
        packs[0] = jnp.where(lane == r, pltpu.roll(first, r, 1), packs[0])
        packs[1] = jnp.where(lane == r, pltpu.roll(last, r + 1, 1), packs[1])

    def halo(sweep, side, arriving):
        slot = opposite[side] if not arriving else side
        if side < 2:
            src = u.at[sweep, 1 if side == 0 else rows]
            dst = u.at[sweep, 0 if slot == 0 else rows + 1]
        else:
            src = edge_out.at[sweep, side - 2]
            dst = edge_in.at[sweep, slot - 2]
        return pltpu.make_async_remote_copy(
            src_ref=src,
            dst_ref=dst,
            send_sem=halo_send.at[sweep, side],
            recv_sem=halo_recv.at[sweep, slot],
            device_id=there[side],
            device_id_type=MESH,
        )

    def exchange(sweep):
        for j in range(2):
            edge_out[sweep, j] = jnp.transpose(packs[j])[:rows]
        for side in (2, 3, 0, 1):

            @pl.when(has[side])
            def _():
                halo(sweep, side, False).start()

        for side in range(4):

            @pl.when(jnp.logical_not(has[side]))
            def _():
                if side < 2:
                    u[sweep, 0 if side == 0 else rows + 1] = jnp.zeros((chans, cols), jnp.float32)
                else:
                    edge_in[sweep, side - 2] = jnp.zeros((rows, chans), jnp.float32)

            @pl.when(has[side])
            def _():
                halo(sweep, side, True).wait_recv()
                halo(sweep, side, False).wait_send()

        for j in range(2):
            filled = jnp.concatenate(
                [edge_in[sweep, j], jnp.zeros((LANES - rows, chans), jnp.float32)], axis=0
            )
            edge_t[j] = jnp.transpose(filled)

    packs[...] = jnp.zeros(packs.shape, jnp.float32)
    sig_copy.wait()
    bal_t = jnp.transpose(balance[...])

    @pl.loop(0, rows)
    def _(r):
        scale = jnp.concatenate(
            [sig[h, pl.ds(r, chans, stride=rows), :] for h in range(halves)], axis=1
        )
        scaled = acc[r] * coef[5, pl.ds(r, 1), :] * scale
        balanced = jnp.dot(
            bal_t, scaled, precision=lax.Precision.HIGHEST, preferred_element_type=jnp.float32
        )
        start = balanced * coef[4, pl.ds(r, 1), :]
        acc[r] = start
        u[0, r + 1] = start
        pack(r, start[:, :LANES], start[:, cols - LANES :])

    for sweep in range(3):
        exchange(sweep)

        @pl.loop(0, rows)
        def _(r):
            mid = u[sweep, r + 1]
            parts = [mid[:, h * LANES : (h + 1) * LANES] for h in range(halves)]
            up = [pltpu.roll(p, 1, 1) for p in parts]
            down = [pltpu.roll(p, LANES - 1, 1) for p in parts]
            before = pltpu.roll(edge_t[0], lax.rem(LANES - r, LANES), 1)
            after = pltpu.roll(edge_t[1], LANES - 1 - r, 1)
            west = [jnp.where(lane == 0, q, p) for p, q in zip(up, [before] + up[:-1])]
            east = [jnp.where(lane == LANES - 1, q, p) for p, q in zip(down, down[1:] + [after])]
            west = jnp.concatenate(west, axis=1)
            east = jnp.concatenate(east, axis=1)
            total = acc[r] + coef[0, pl.ds(r, 1), :] * u[sweep, r]
            total = total + coef[1, pl.ds(r, 1), :] * u[sweep, r + 2]
            total = total + coef[2, pl.ds(r, 1), :] * west
            total = total + coef[3, pl.ds(r, 1), :] * east
            if sweep < 2:
                u[sweep + 1, r + 1] = total
                pack(r, total[:, :LANES], total[:, cols - LANES :])
            else:
                out[r] = total

    @pl.loop(1, tiles)
    def _(k):
        item_copy(lax.rem(me + k, tiles), me).wait_send()


def on_device(
    innovation,
    fractions,
    owner,
    obs_row,
    obs_col,
    obs_field,
    obs_level,
    land_mask,
    kappa,
    sigma,
    balance,
):
    n_lon = lax.axis_size("lon")
    n_lat = lax.axis_size("lat")
    tiles = n_lon * n_lat
    obs = innovation.shape[0]
    slots = 2 * obs // tiles
    chans, rows, cols = sigma.shape
    halves = cols // LANES
    depth = min(1024, tiles * slots)
    line = lambda x: x.reshape(1, obs)
    vmem = pl.BlockSpec(memory_space=pltpu.VMEM)
    f32 = jnp.float32
    sig_lines = jnp.transpose(sigma.reshape(chans * rows, halves, LANES), (1, 0, 2))
    field = pl.pallas_call(
        functools.partial(kernel, n_lon, n_lat),
        out_shape=jax.ShapeDtypeStruct((rows, chans, cols), f32),
        in_specs=[vmem] * 10 + [pl.BlockSpec(memory_space=pl.ANY)],
        out_specs=vmem,
        scratch_shapes=[
            pltpu.VMEM((halves, chans * rows, LANES), f32),
            pltpu.VMEM((tiles, 8, slots), f32),
            pltpu.VMEM((tiles, 8, slots), f32),
            pltpu.VMEM((2, rows, cols), f32),
            pltpu.VMEM((4, 2, rows, cols), f32),
            pltpu.VMEM((6, rows, cols), f32),
            pltpu.VMEM((chans, depth), f32),
            pltpu.VMEM((rows, depth), f32),
            pltpu.VMEM((cols, depth), jnp.bfloat16),
            pltpu.VMEM((cols, depth), jnp.bfloat16),
            pltpu.VMEM((rows, chans, cols), f32),
            pltpu.VMEM((3, rows + 2, chans, cols), f32),
            pltpu.VMEM((3, 2, rows, chans), f32),
            pltpu.VMEM((3, 2, rows, chans), f32),
            pltpu.VMEM((2, chans, LANES), f32),
            pltpu.VMEM((2, chans, LANES), f32),
            pltpu.SemaphoreType.DMA,
            pltpu.SemaphoreType.DMA((tiles,)),
            pltpu.SemaphoreType.DMA((tiles,)),
            pltpu.SemaphoreType.DMA((4,)),
            pltpu.SemaphoreType.DMA((4,)),
            pltpu.SemaphoreType.DMA((3, 4)),
            pltpu.SemaphoreType.DMA((3, 4)),
        ],
        compiler_params=pltpu.CompilerParams(
            collective_id=0, has_side_effects=True, vmem_limit_bytes=56 * 1024 * 1024
        ),
    )(
        line(innovation),
        fractions,
        line(owner),
        line(obs_row),
        line(obs_col),
        line(obs_field),
        line(obs_level),
        land_mask,
        kappa,
        balance,
        sig_lines,
    )
    return jnp.transpose(field, (1, 0, 2))


def solution(mesh):
    spread = P(("member", "lon", "lat"))
    in_specs = (
        spread,
        P(None, ("member", "lon", "lat")),
        P(("member", "lon", "lat"), None),
        spread,
        spread,
        spread,
        spread,
        P("lat", "lon"),
        P("lat", "lon"),
        P(None, "lat", "lon"),
        P(),
    )
    out_specs = P("member", "lat", "lon")
    return jax.shard_map(
        on_device, mesh=mesh, in_specs=in_specs, out_specs=out_specs, check_vma=False
    )
```

time: 207 us -> 64.2 us (0.31)
  other arithmetic: 70.3 us -> 0 us
  Pallas kernels: 0 us -> 56.1 us
  matrix products: 55 us -> 0 us
  starting transfers between devices: 40.1 us -> 0 us
  waiting for transfers between devices: 30.9 us -> 0 us
    pallas_call x0 -> x1, Pallas kernels: none -> 56.1 us  [on_device(): pl.pallas_call(functools.partial(kernel, n_lon, n_lat), out_shape=jax.Sha...]
    dot_general x7 -> x0, matrix products: 55 us -> none  [the longest x4 50.1 us: accumulate(): jnp.dot(jnp.concatenate(lefts, axis=1), jnp.concatenate(rights, axis=0),...]
    add x17 -> x0, other arithmetic: 38 us -> none  [the longest x4 37.8 us: accumulate(): left + jnp.where(row_ids == target[None, :], term_blk[lz * 4 + dy * 2 + d...]
    ppermute x16 -> x0, starting transfers between devices: 28.9 us -> none  [the longest x8 18.6 us: with_halo(): lax.ppermute(tail, axis, [(i, (i + 1) % count) for i in range(ends)])]
    div x4 -> x0, other arithmetic: 21.7 us -> none  [the longest x3 20.4 us: relax(): return total / denom]
    ppermute x16 -> x0, waiting for transfers between devices: 17.7 us -> none  [the longest x8 17.6 us: with_halo(): lax.ppermute(head, axis, [((i + 1) % count, i) for i in range(ends)])]
    all_to_all x2 -> x0, waiting for transfers between devices: 13.2 us -> none  [the longest x1 7.55 us: on_device(): lax.all_to_all(float_buckets, ('lon', 'lat'), split_axis=1, concat_axis=1...]
    all_to_all x2 -> x0, starting transfers between devices: 11.1 us -> none  [the longest x1 7.62 us: on_device(): lax.all_to_all(int_buckets, ('lon', 'lat'), split_axis=1, concat_axis=1,...]
  transfers between devices with their start and end apart: 18 -> 0, of which waited for: 8 -> 0; matrix products, arithmetic and copies ran while one was open for 4% -> 0% of each run, Pallas kernels for 0% -> 0%
where the time goes in v1:
time: 64.2 us; the launch traced here: 64 us
  Pallas kernels  56.1 us (87%)
  local copies, waits for them, and re-layouts  7.87 us (12%)
    pallas_call x1, Pallas kernels, on_device(): pl.pallas_call(functools.partial(kernel, n_lon, n_lat), out_shape=jax.Sha...  56.1 us
    transpose x1, local copies, waits for them, and re-layouts, on_device(): return jnp.transpose(field, (1, 0, 2))  4.13 us
    reshape x2, local copies, waits for them, and re-layouts, on_device(): sigma.reshape(chans * rows, halves, LANES)  3.75 us

profile of v1, /device:TPU:0, one launch (start us, length us, event | category | flops | bytes accessed | tf_op | source)
XLA Modules:
  0.0 64.0 jit_solution(9331750477987928147)
XLA Ops:
  0.0 2.3 %reshape.27 = f32[2048,2,128]{2,1,0:T(2,128)S(1)} reshape(f32[128,16,256]{2,1,0:T(8,128)} %param.20) | data formatting | bytes 4194304 | tf_op jit(solution)/shard_map/reshape | solution.py:368
  2.3 1.5 %copy.16 = f32[2048,2,128]{2,0,1:T(8,128)} copy(f32[2048,2,128]{2,1,0:T(2,128)S(1)} %reshape.27) | data formatting | bytes 4194304 | tf_op jit(solution)/shard_map/reshape | solution.py:368
  3.8 56.1 %shard_map.109 = f32[16,128,256]{2,1,0:T(8,128)} custom-call(f32[1,2048]{1,0:T(1,128)} %bitcast.12, f32[3,2048]{1,0:T(4,128)} %frac.1, s32[1,2048]{1,0:T(1,128)} %bitcast.13, s32[1,2048]{1,0:T(1,128)} %bitcast.14, s32[1,2048]{1,0:T(1,128)} %bitcast.15, s32[1,2048]{1,0:T(1,128)} %bitcast.16, s32[1,2048]{1,0:T(1,128)} %bitcast.17, s32[16,256]{1,0:T(8,128)} %mask.1, ...), custom_call_target="tpu_custom_call" | custom-call | tf_op jit(solution)/shard_map/pallas_call | solution.py:369
  59.9 4.1 %copy.14 = f32[128,16,256]{2,1,0:T(8,128)} copy(f32[128,16,256]{2,0,1:T(8,128)} %bitcast.11) | data formatting | bytes 4194304 | tf_op jit(solution)/shard_map/transpose | solution.py:415

commit v2 on v1

--- a/solution.py
+++ b/solution.py
@@ -12,6 +12,7 @@
 MESH = pl.DeviceIdType.MESH
 NT = (((1,), (1,)), ((), ()))
 LANES = 128
+BAND = 8
 
 
 def iota_f(shape, dim):
@@ -25,6 +26,15 @@
 def split2(x):
     hi = x.astype(jnp.bfloat16)
     return hi, (x - hi.astype(jnp.float32)).astype(jnp.bfloat16)
+
+
+def turn(x, shift):
+    shift = shift % LANES
+    return pltpu.roll(x, shift, 1) if shift else x
+
+
+def pack(lane, r, source, held, values):
+    return jnp.where(lane == r, turn(values, r - source), held)
 
 
 def buckets(innov, frac, owner, orow, ocol, ofield, olev, tiles, slots):
@@ -108,8 +118,12 @@
     def where_is(tile):
         return {"lon": tile // n_lat, "lat": lax.rem(tile, n_lat)}
 
-    sig_copy = pltpu.make_async_copy(sigma, sig, sig_sem)
-    sig_copy.start()
+    sig_copies = [
+        pltpu.make_async_copy(sigma.at[:, pl.ds(h * LANES, LANES)], sig.at[h], sig_sem.at[h])
+        for h in range(halves)
+    ]
+    for copy in sig_copies:
+        copy.start()
     barrier = pltpu.get_barrier_semaphore()
 
     @pl.loop(1, tiles)
@@ -240,12 +254,6 @@
         coef[side] = faces[side] * inv
     coef[4] = inv
     coef[5] = mc
-
-    lane = lax.broadcasted_iota(jnp.int32, (chans, LANES), 1)
-
-    def pack(r, first, last):
-        packs[0] = jnp.where(lane == r, pltpu.roll(first, r, 1), packs[0])
-        packs[1] = jnp.where(lane == r, pltpu.roll(last, r + 1, 1), packs[1])
 
     def halo(sweep, side, arriving):
         slot = opposite[side] if not arriving else side
@@ -293,52 +301,99 @@
             )
             edge_t[j] = jnp.transpose(filled)
 
-    packs[...] = jnp.zeros(packs.shape, jnp.float32)
-    sig_copy.wait()
-    bal_t = jnp.transpose(balance[...])
-
-    @pl.loop(0, rows)
-    def _(r):
-        scale = jnp.concatenate(
-            [sig[h, pl.ds(r, chans, stride=rows), :] for h in range(halves)], axis=1
-        )
-        scaled = acc[r] * coef[5, pl.ds(r, 1), :] * scale
+    for copy in sig_copies:
+        copy.wait()
+    bal_hi, bal_lo = split2(jnp.transpose(balance[...]))
+    bal_twice = jnp.concatenate([bal_hi, bal_hi], axis=1)
+
+    @pl.loop(0, rows // step_rows)
+    def _(part):
+        lines = [part * step_rows + j for j in range(step_rows)]
+        scaled = []
+        for r in lines:
+            scale = jnp.concatenate(
+                [sig[h, pl.ds(r, chans, stride=rows), :] for h in range(halves)], axis=1
+            )
+            scaled.append(acc[r] * coef[5, pl.ds(r, 1), :] * scale)
+        hi, lo = split2(jnp.concatenate(scaled, axis=1))
         balanced = jnp.dot(
-            bal_t, scaled, precision=lax.Precision.HIGHEST, preferred_element_type=jnp.float32
-        )
-        start = balanced * coef[4, pl.ds(r, 1), :]
-        acc[r] = start
-        u[0, r + 1] = start
-        pack(r, start[:, :LANES], start[:, cols - LANES :])
+            bal_twice, jnp.concatenate([hi, lo], axis=0), preferred_element_type=jnp.float32
+        ) + jnp.dot(bal_lo, hi, preferred_element_type=jnp.float32)
+        for j, r in enumerate(lines):
+            start = balanced[:, j * cols : (j + 1) * cols] * coef[4, pl.ds(r, 1), :]
+            acc[r] = start
+            u[0, r + 1] = start
+
+    lane = lax.broadcasted_iota(jnp.int32, (BAND, LANES), 1)
+
+    @pl.loop(0, chans // BAND)
+    def _(band):
+        here = pl.ds(pl.multiple_of(band * BAND, BAND), BAND)
+        first = jnp.zeros((BAND, LANES), jnp.float32)
+        last = jnp.zeros((BAND, LANES), jnp.float32)
+        for r in range(rows):
+            first = pack(lane, r, 0, first, acc[r, here, :LANES])
+            last = pack(lane, r, LANES - 1, last, acc[r, here, cols - LANES :])
+        packs[0, here] = first
+        packs[1, here] = last
 
     for sweep in range(3):
         exchange(sweep)
 
-        @pl.loop(0, rows)
-        def _(r):
-            mid = u[sweep, r + 1]
-            parts = [mid[:, h * LANES : (h + 1) * LANES] for h in range(halves)]
-            up = [pltpu.roll(p, 1, 1) for p in parts]
-            down = [pltpu.roll(p, LANES - 1, 1) for p in parts]
-            before = pltpu.roll(edge_t[0], lax.rem(LANES - r, LANES), 1)
-            after = pltpu.roll(edge_t[1], LANES - 1 - r, 1)
-            west = [jnp.where(lane == 0, q, p) for p, q in zip(up, [before] + up[:-1])]
-            east = [jnp.where(lane == LANES - 1, q, p) for p, q in zip(down, down[1:] + [after])]
-            west = jnp.concatenate(west, axis=1)
-            east = jnp.concatenate(east, axis=1)
-            total = acc[r] + coef[0, pl.ds(r, 1), :] * u[sweep, r]
-            total = total + coef[1, pl.ds(r, 1), :] * u[sweep, r + 2]
-            total = total + coef[2, pl.ds(r, 1), :] * west
-            total = total + coef[3, pl.ds(r, 1), :] * east
+        @pl.loop(0, chans // BAND)
+        def _(band):
+            here = pl.ds(pl.multiple_of(band * BAND, BAND), BAND)
+            edges = (edge_t[0, here], edge_t[1, here])
+            first = jnp.zeros((BAND, LANES), jnp.float32)
+            last = jnp.zeros((BAND, LANES), jnp.float32)
+
+            def line(r):
+                return [u[sweep, r, here, h * LANES : (h + 1) * LANES] for h in range(halves)]
+
+            south, mid = line(0), line(1)
+            for r in range(rows):
+                north = line(r + 2)
+                up = [pltpu.roll(p, 1, 1) for p in mid]
+                down = [pltpu.roll(p, LANES - 1, 1) for p in mid]
+                before = turn(edges[0], -r)
+                after = turn(edges[1], LANES - 1 - r)
+                west = [jnp.where(lane == 0, q, p) for p, q in zip(up, [before] + up[:-1])]
+                east = [
+                    jnp.where(lane == LANES - 1, q, p) for p, q in zip(down, down[1:] + [after])
+                ]
+                totals = []
+                for h in range(halves):
+                    part = pl.ds(h * LANES, LANES)
+                    total = acc[r, here, part] + coef[0, r : r + 1, part] * south[h]
+                    total = total + coef[1, r : r + 1, part] * north[h]
+                    total = total + coef[2, r : r + 1, part] * west[h]
+                    total = total + coef[3, r : r + 1, part] * east[h]
+                    totals.append(total)
+                    if sweep < 2:
+                        u[sweep + 1, r + 1, here, part] = total
+                    else:
+                        sig[h, pl.ds(band * BAND * rows + r, BAND, stride=rows), :] = total
+                if sweep < 2:
+                    first = pack(lane, r, 0, first, totals[0])
+                    last = pack(lane, r, LANES - 1, last, totals[-1])
+                south, mid = mid, north
             if sweep < 2:
-                u[sweep + 1, r + 1] = total
-                pack(r, total[:, :LANES], total[:, cols - LANES :])
-            else:
-                out[r] = total
+                packs[0, here] = first
+                packs[1, here] = last
+
+    out_copies = [
+        pltpu.make_async_copy(sig.at[h], out.at[:, pl.ds(h * LANES, LANES)], sig_sem.at[h])
+        for h in range(halves)
+    ]
+    for copy in out_copies:
+        copy.start()
 
     @pl.loop(1, tiles)
     def _(k):
         item_copy(lax.rem(me + k, tiles), me).wait_send()
+
+    for copy in out_copies:
+        copy.wait()
 
 
 def on_device(
@@ -365,12 +420,11 @@
     line = lambda x: x.reshape(1, obs)
     vmem = pl.BlockSpec(memory_space=pltpu.VMEM)
     f32 = jnp.float32
-    sig_lines = jnp.transpose(sigma.reshape(chans * rows, halves, LANES), (1, 0, 2))
     field = pl.pallas_call(
         functools.partial(kernel, n_lon, n_lat),
-        out_shape=jax.ShapeDtypeStruct((rows, chans, cols), f32),
+        out_shape=jax.ShapeDtypeStruct((chans * rows, cols), f32),
         in_specs=[vmem] * 10 + [pl.BlockSpec(memory_space=pl.ANY)],
-        out_specs=vmem,
+        out_specs=pl.BlockSpec(memory_space=pl.ANY),
         scratch_shapes=[
             pltpu.VMEM((halves, chans * rows, LANES), f32),
             pltpu.VMEM((tiles, 8, slots), f32),
@@ -388,7 +442,7 @@
             pltpu.VMEM((3, 2, rows, chans), f32),
             pltpu.VMEM((2, chans, LANES), f32),
             pltpu.VMEM((2, chans, LANES), f32),
-            pltpu.SemaphoreType.DMA,
+            pltpu.SemaphoreType.DMA((halves,)),
             pltpu.SemaphoreType.DMA((tiles,)),
             pltpu.SemaphoreType.DMA((tiles,)),
             pltpu.SemaphoreType.DMA((4,)),
@@ -410,9 +464,9 @@
         land_mask,
         kappa,
         balance,
-        sig_lines,
+        sigma.reshape(chans * rows, cols),
     )
-    return jnp.transpose(field, (1, 0, 2))
+    return field.reshape(chans, rows, cols)
 
 
 def solution(mesh):

time: 64.2 us -> 58.4 us (0.910)
  local copies, waits for them, and re-layouts: 7.87 us -> 3.08 us
  Pallas kernels: 56.1 us -> 55.1 us
    transpose x1 -> x0, local copies, waits for them, and re-layouts: 4.13 us -> none  [on_device(): return jnp.transpose(field, (1, 0, 2))]
    reshape x2 -> x0, local copies, waits for them, and re-layouts: 3.75 us -> none  [on_device(): sigma.reshape(chans * rows, halves, LANES)]
    unnamed x0 -> x1, local copies, waits for them, and re-layouts: none -> 3.08 us
    pallas_call x1, Pallas kernels: 56.1 us -> 55.1 us  [on_device(): pl.pallas_call(functools.partial(kernel, n_lon, n_lat), out_shape=jax.Sha...]
where the time goes in v2:
time: 58.4 us; the launch traced here: 58.2 us
  Pallas kernels  55.1 us (94%)
  local copies, waits for them, and re-layouts  3.08 us (5%)
    pallas_call x1, Pallas kernels, on_device(): pl.pallas_call(functools.partial(kernel, n_lon, n_lat), out_shape=jax.Sha...  55.1 us
    unnamed x1, local copies, waits for them, and re-layouts  3.08 us

profile of v2, /device:TPU:0, one launch (start us, length us, event | category | flops | bytes accessed | tf_op | source)
XLA Modules:
  0.0 58.2 jit_solution(3248026857400697961)
XLA Ops:
  0.0 55.1 %shard_map.109 = f32[2048,256]{1,0:T(8,128)} custom-call(f32[1,2048]{1,0:T(1,128)} %bitcast.10, f32[3,2048]{1,0:T(4,128)} %frac.1, s32[1,2048]{1,0:T(1,128)} %bitcast.11, s32[1,2048]{1,0:T(1,128)} %bitcast.12, s32[1,2048]{1,0:T(1,128)} %bitcast.13, s32[1,2048]{1,0:T(1,128)} %bitcast.14, s32[1,2048]{1,0:T(1,128)} %bitcast.15, s32[16,256]{1,0:T(8,128)} %mask.1, ...), custom_call_target="tpu_custom_call" | custom-call | tf_op jit(solution)/shard_map/pallas_call | solution.py:423
  55.1 3.1 %copy.13 = f32[128,16,256]{2,1,0:T(8,128)} copy(f32[128,16,256]{2,1,0:T(8,128)} %bitcast.8) | data formatting | bytes 4194304

commit v3 on v2

--- a/solution.py
+++ b/solution.py
@@ -13,6 +13,9 @@
 NT = (((1,), (1,)), ((), ()))
 LANES = 128
 BAND = 8
+GROUPS = 2
+F8 = jnp.float8_e4m3fn
+LIFT = 512.0
 
 
 def iota_f(shape, dim):
@@ -33,8 +36,9 @@
     return pltpu.roll(x, shift, 1) if shift else x
 
 
-def pack(lane, r, source, held, values):
-    return jnp.where(lane == r, turn(values, r - source), held)
+def pack(lane, r, held, first, last):
+    both = turn(jnp.where(lane == LANES - 1, last, first), 2 * r + 1)
+    return jnp.where((lane == 2 * r) | (lane == 2 * r + 1), both, held)
 
 
 def buckets(innov, frac, owner, orow, ocol, ofield, olev, tiles, slots):
@@ -91,7 +95,7 @@
     a_ref,
     b_ref,
     r_hi,
-    r_lo,
+    r_fix,
     acc,
     u,
     edge_out,
@@ -214,20 +218,25 @@
         ch, row, col = items[4:5], items[5:6], items[6:7]
         a_ref[...] = hat(iota_f((chans, depth), 0), ch, val * (1.0 - fz), val * fz)
         b_ref[...] = hat(iota_f((rows, depth), 0), row, 1.0 - fy, fy)
-        hi, lo = split2(hat(iota_f((cols, depth), 0), col, 1.0 - fx, fx))
+        right = hat(iota_f((cols, depth), 0), col, 1.0 - fx, fx)
+        hi = right.astype(jnp.bfloat16)
         r_hi[...] = hi
-        r_lo[...] = lo
+        r_fix[:, :depth] = right.astype(F8)
+        r_fix[:, depth:] = ((right - hi.astype(jnp.float32)) * LIFT).astype(F8)
 
         @pl.loop(0, rows // step_rows)
         def _(part):
             lefts = [
                 a_ref[...] * b_ref[pl.ds(part * step_rows + j, 1), :] for j in range(step_rows)
             ]
-            left_hi, left_lo = split2(jnp.concatenate(lefts, axis=0))
+            left = jnp.concatenate(lefts, axis=0)
+            left_hi = left.astype(jnp.bfloat16)
+            left_lo = ((left - left_hi.astype(jnp.float32)) * LIFT).astype(F8)
+            left_fix = jnp.concatenate([left_lo, left.astype(F8)], axis=1)
             dot = functools.partial(
                 lax.dot_general, dimension_numbers=NT, preferred_element_type=jnp.float32
             )
-            total = dot(left_hi, r_hi[...]) + dot(left_lo, r_hi[...]) + dot(left_hi, r_lo[...])
+            total = dot(left_hi, r_hi[...]) + dot(left_fix, r_fix[...]) * (1.0 / LIFT)
             here = pl.ds(pl.multiple_of(part * step_rows, step_rows), step_rows)
             acc[here] += total.reshape(step_rows, chans, cols)
 
@@ -255,51 +264,58 @@
     coef[4] = inv
     coef[5] = mc
 
-    def halo(sweep, side, arriving):
+    width = chans // GROUPS
+
+    def halo(sweep, group, side, arriving):
         slot = opposite[side] if not arriving else side
         if side < 2:
-            src = u.at[sweep, 1 if side == 0 else rows]
-            dst = u.at[sweep, 0 if slot == 0 else rows + 1]
+            part = pl.ds(group * width, width)
+            src = u.at[sweep, 1 if side == 0 else rows, part]
+            dst = u.at[sweep, 0 if slot == 0 else rows + 1, part]
         else:
-            src = edge_out.at[sweep, side - 2]
-            dst = edge_in.at[sweep, slot - 2]
+            src = edge_out.at[sweep, group]
+            dst = edge_in.at[sweep, group, slot - 2]
         return pltpu.make_async_remote_copy(
             src_ref=src,
             dst_ref=dst,
-            send_sem=halo_send.at[sweep, side],
-            recv_sem=halo_recv.at[sweep, slot],
+            send_sem=halo_send.at[sweep, group, side],
+            recv_sem=halo_recv.at[sweep, group, slot],
             device_id=there[side],
             device_id_type=MESH,
         )
 
-    def exchange(sweep):
-        for j in range(2):
-            edge_out[sweep, j] = jnp.transpose(packs[j])[:rows]
+    def give(sweep, group):
+        part = pl.ds(group * width, width)
+        edge_out[sweep, group] = jnp.transpose(packs[part])[: 2 * rows]
         for side in (2, 3, 0, 1):
 
             @pl.when(has[side])
             def _():
-                halo(sweep, side, False).start()
-
-        for side in range(4):
+                halo(sweep, group, side, False).start()
 
             @pl.when(jnp.logical_not(has[side]))
             def _():
                 if side < 2:
-                    u[sweep, 0 if side == 0 else rows + 1] = jnp.zeros((chans, cols), jnp.float32)
+                    u[sweep, 0 if side == 0 else rows + 1, part] = jnp.zeros(
+                        (width, cols), jnp.float32
+                    )
                 else:
-                    edge_in[sweep, side - 2] = jnp.zeros((rows, chans), jnp.float32)
+                    edge_in[sweep, group, side - 2] = jnp.zeros((2 * rows, width), jnp.float32)
+
+    def take(sweep, group):
+        for side in range(4):
 
             @pl.when(has[side])
             def _():
-                halo(sweep, side, True).wait_recv()
-                halo(sweep, side, False).wait_send()
-
-        for j in range(2):
-            filled = jnp.concatenate(
-                [edge_in[sweep, j], jnp.zeros((LANES - rows, chans), jnp.float32)], axis=0
-            )
-            edge_t[j] = jnp.transpose(filled)
+                halo(sweep, group, side, True).wait_recv()
+
+        odd = lax.broadcasted_iota(jnp.int32, (2 * rows, width), 0) % 2 == 1
+        west = pltpu.roll(edge_in[sweep, group, 0], 1, 0)
+        east = pltpu.roll(edge_in[sweep, group, 1], 2 * rows - 1, 0)
+        filled = jnp.concatenate(
+            [jnp.where(odd, west, east), jnp.zeros((LANES - 2 * rows, width), jnp.float32)], axis=0
+        )
+        edge_t[pl.ds(group * width, width)] = jnp.transpose(filled)
 
     for copy in sig_copies:
         copy.wait()
@@ -326,26 +342,27 @@
 
     lane = lax.broadcasted_iota(jnp.int32, (BAND, LANES), 1)
 
-    @pl.loop(0, chans // BAND)
-    def _(band):
-        here = pl.ds(pl.multiple_of(band * BAND, BAND), BAND)
-        first = jnp.zeros((BAND, LANES), jnp.float32)
-        last = jnp.zeros((BAND, LANES), jnp.float32)
-        for r in range(rows):
-            first = pack(lane, r, 0, first, acc[r, here, :LANES])
-            last = pack(lane, r, LANES - 1, last, acc[r, here, cols - LANES :])
-        packs[0, here] = first
-        packs[1, here] = last
-
-    for sweep in range(3):
-        exchange(sweep)
-
-        @pl.loop(0, chans // BAND)
+    bands = width // BAND
+    for group in range(GROUPS):
+
+        @pl.loop(group * bands, (group + 1) * bands)
         def _(band):
             here = pl.ds(pl.multiple_of(band * BAND, BAND), BAND)
-            edges = (edge_t[0, here], edge_t[1, here])
-            first = jnp.zeros((BAND, LANES), jnp.float32)
-            last = jnp.zeros((BAND, LANES), jnp.float32)
+            held = jnp.zeros((BAND, LANES), jnp.float32)
+            for r in range(rows):
+                held = pack(lane, r, held, acc[r, here, :LANES], acc[r, here, cols - LANES :])
+            packs[here] = held
+
+        give(0, group)
+
+    for sweep, group in [(sweep, group) for sweep in range(3) for group in range(GROUPS)]:
+        take(sweep, group)
+
+        @pl.loop(group * bands, (group + 1) * bands)
+        def _(band):
+            here = pl.ds(pl.multiple_of(band * BAND, BAND), BAND)
+            edges = edge_t[here]
+            held = jnp.zeros((BAND, LANES), jnp.float32)
 
             def line(r):
                 return [u[sweep, r, here, h * LANES : (h + 1) * LANES] for h in range(halves)]
@@ -355,11 +372,10 @@
                 north = line(r + 2)
                 up = [pltpu.roll(p, 1, 1) for p in mid]
                 down = [pltpu.roll(p, LANES - 1, 1) for p in mid]
-                before = turn(edges[0], -r)
-                after = turn(edges[1], LANES - 1 - r)
-                west = [jnp.where(lane == 0, q, p) for p, q in zip(up, [before] + up[:-1])]
+                outer = turn(edges, -(2 * r + 1))
+                west = [jnp.where(lane == 0, q, p) for p, q in zip(up, [outer] + up[:-1])]
                 east = [
-                    jnp.where(lane == LANES - 1, q, p) for p, q in zip(down, down[1:] + [after])
+                    jnp.where(lane == LANES - 1, q, p) for p, q in zip(down, down[1:] + [outer])
                 ]
                 totals = []
                 for h in range(halves):
@@ -374,12 +390,13 @@
                     else:
                         sig[h, pl.ds(band * BAND * rows + r, BAND, stride=rows), :] = total
                 if sweep < 2:
-                    first = pack(lane, r, 0, first, totals[0])
-                    last = pack(lane, r, LANES - 1, last, totals[-1])
+                    held = pack(lane, r, held, totals[0], totals[-1])
                 south, mid = mid, north
             if sweep < 2:
-                packs[0, here] = first
-                packs[1, here] = last
+                packs[here] = held
+
+        if sweep < 2:
+            give(sweep + 1, group)
 
     out_copies = [
         pltpu.make_async_copy(sig.at[h], out.at[:, pl.ds(h * LANES, LANES)], sig_sem.at[h])
@@ -391,6 +408,14 @@
     @pl.loop(1, tiles)
     def _(k):
         item_copy(lax.rem(me + k, tiles), me).wait_send()
+
+    for sweep, group, side in [
+        (a, b, c) for a in range(3) for b in range(GROUPS) for c in range(4)
+    ]:
+
+        @pl.when(has[side])
+        def _():
+            halo(sweep, group, side, False).wait_send()
 
     for copy in out_copies:
         copy.wait()
@@ -435,20 +460,20 @@
             pltpu.VMEM((chans, depth), f32),
             pltpu.VMEM((rows, depth), f32),
             pltpu.VMEM((cols, depth), jnp.bfloat16),
-            pltpu.VMEM((cols, depth), jnp.bfloat16),
+            pltpu.VMEM((cols, 2 * depth), F8),
             pltpu.VMEM((rows, chans, cols), f32),
             pltpu.VMEM((3, rows + 2, chans, cols), f32),
-            pltpu.VMEM((3, 2, rows, chans), f32),
-            pltpu.VMEM((3, 2, rows, chans), f32),
-            pltpu.VMEM((2, chans, LANES), f32),
-            pltpu.VMEM((2, chans, LANES), f32),
+            pltpu.VMEM((3, GROUPS, 2 * rows, chans // GROUPS), f32),
+            pltpu.VMEM((3, GROUPS, 2, 2 * rows, chans // GROUPS), f32),
+            pltpu.VMEM((chans, LANES), f32),
+            pltpu.VMEM((chans, LANES), f32),
             pltpu.SemaphoreType.DMA((halves,)),
             pltpu.SemaphoreType.DMA((tiles,)),
             pltpu.SemaphoreType.DMA((tiles,)),
             pltpu.SemaphoreType.DMA((4,)),
             pltpu.SemaphoreType.DMA((4,)),
-            pltpu.SemaphoreType.DMA((3, 4)),
-            pltpu.SemaphoreType.DMA((3, 4)),
+            pltpu.SemaphoreType.DMA((3, GROUPS, 4)),
+            pltpu.SemaphoreType.DMA((3, GROUPS, 4)),
         ],
         compiler_params=pltpu.CompilerParams(
             collective_id=0, has_side_effects=True, vmem_limit_bytes=56 * 1024 * 1024

time: 58.4 us -> 49.9 us (0.85)
  Pallas kernels: 55.1 us -> 46.7 us
    pallas_call x1, Pallas kernels: 55.1 us -> 46.7 us  [on_device(): pl.pallas_call(functools.partial(kernel, n_lon, n_lat), out_shape=jax.Sha...]
where the time goes in v3:
time: 49.9 us; the launch traced here: 49.8 us
  Pallas kernels  46.7 us (94%)
  local copies, waits for them, and re-layouts  3.08 us (6%)
    pallas_call x1, Pallas kernels, on_device(): pl.pallas_call(functools.partial(kernel, n_lon, n_lat), out_shape=jax.Sha...  46.7 us
    unnamed x1, local copies, waits for them, and re-layouts  3.08 us

profile of v3, /device:TPU:0, one launch (start us, length us, event | category | flops | bytes accessed | tf_op | source)
XLA Modules:
  0.0 49.8 jit_solution(17689423392090031026)
XLA Ops:
  0.0 46.7 %shard_map.109 = f32[2048,256]{1,0:T(8,128)} custom-call(f32[1,2048]{1,0:T(1,128)} %bitcast.10, f32[3,2048]{1,0:T(4,128)} %frac.1, s32[1,2048]{1,0:T(1,128)} %bitcast.11, s32[1,2048]{1,0:T(1,128)} %bitcast.12, s32[1,2048]{1,0:T(1,128)} %bitcast.13, s32[1,2048]{1,0:T(1,128)} %bitcast.14, s32[1,2048]{1,0:T(1,128)} %bitcast.15, s32[16,256]{1,0:T(8,128)} %mask.1, ...), custom_call_target="tpu_custom_call" | custom-call | tf_op jit(solution)/shard_map/pallas_call | solution.py:448
  46.7 3.1 %copy.13 = f32[128,16,256]{2,1,0:T(8,128)} copy(f32[128,16,256]{2,1,0:T(8,128)} %bitcast.8) | data formatting | bytes 4194304

commit v4 on v3

--- a/solution.py
+++ b/solution.py
@@ -198,7 +198,7 @@
     recv[me] = send[me]
     acc[...] = jnp.zeros(acc.shape, jnp.float32)
     group = a_ref.shape[1] // slots
-    step_rows = math.gcd(rows, 4)
+    step_rows = math.gcd(rows, 8)
 
     @pl.loop(0, tiles // group)
     def _(chunk):

time: 49.9 us -> 48.2 us (0.966)
  Pallas kernels: 46.7 us -> 45 us
    pallas_call x1, Pallas kernels: 46.7 us -> 45 us  [on_device(): pl.pallas_call(functools.partial(kernel, n_lon, n_lat), out_shape=jax.Sha...]
where the time goes in v4:
time: 48.2 us; the launch traced here: 48.1 us
  Pallas kernels  45 us (93%)
  local copies, waits for them, and re-layouts  3.08 us (6%)
    pallas_call x1, Pallas kernels, on_device(): pl.pallas_call(functools.partial(kernel, n_lon, n_lat), out_shape=jax.Sha...  45 us
    unnamed x1, local copies, waits for them, and re-layouts  3.08 us

profile of v4, /device:TPU:0, one launch (start us, length us, event | category | flops | bytes accessed | tf_op | source)
XLA Modules:
  0.0 48.1 jit_solution(18236216424755189364)
XLA Ops:
  0.0 45.0 %shard_map.109 = f32[2048,256]{1,0:T(8,128)} custom-call(f32[1,2048]{1,0:T(1,128)} %bitcast.10, f32[3,2048]{1,0:T(4,128)} %frac.1, s32[1,2048]{1,0:T(1,128)} %bitcast.11, s32[1,2048]{1,0:T(1,128)} %bitcast.12, s32[1,2048]{1,0:T(1,128)} %bitcast.13, s32[1,2048]{1,0:T(1,128)} %bitcast.14, s32[1,2048]{1,0:T(1,128)} %bitcast.15, s32[16,256]{1,0:T(8,128)} %mask.1, ...), custom_call_target="tpu_custom_call" | custom-call | tf_op jit(solution)/shard_map/pallas_call | solution.py:448
  45.0 3.1 %copy.13 = f32[128,16,256]{2,1,0:T(8,128)} copy(f32[128,16,256]{2,1,0:T(8,128)} %bitcast.8) | data formatting | bytes 4194304
